TPU v7x, 32 devices: a whole 2x2x4 slice. The times are simulated.
32 devices in a mesh: gx: 4 (over z), gy: 4 (over y, x), af: 2 (over core).
Axes of the slice: x: 2, y: 2, z: 4, core: 2. Of those that a mesh axis runs over, the one named last changes fastest.
Arguments:
- activations: bfloat16 [64, 8, 32, 128], P('af', 'gx', 'gy'), may hold values from -6 to 6
- filters: bfloat16 [3, 3, 3, 64, 64], P(None, None, None, 'af'), may hold values from -0.15625 to 0.15625
- conv_bias: float32 [64], P('af'), may hold values from -3 to 3
- grad_output: bfloat16 [64, 8, 32, 128], P('af', 'gx', 'gy'), may hold values from -23 to 23
Outputs:
- input_grads: bfloat16 [64, 8, 32, 128], P('af', 'gx', 'gy')
- filter_grads: float32 [3, 3, 3, 64, 64], P(None, None, None, 'af')
- bias_grads: float32 [64], P('af')
All inputs are finite; a program needn't handle non-finite values.
Results may differ from a plain program's by a relative error of at most 0.0095.
Values may be sent and summed in bfloat16 or wider, within the bound.
A program may use at most 64 MiB of HBM per device.

v0:
```python
import functools
import math

import jax
import jax.numpy as jnp
from jax import lax
from jax.experimental import pallas as pl
from jax.experimental.pallas import tpu as pltpu
from jax.sharding import PartitionSpec as P

MESH = pl.DeviceIdType.MESH
F32, BF16 = jnp.float32, jnp.bfloat16
SIDES = [(dx, dy) for dx in (-1, 0, 1) for dy in (-1, 0, 1) if (dx, dy) != (0, 0)]


def kernel(sizes, act_hbm, filt_hbm, bias_hbm, gout_hbm, igrad_ref, fgrad_ref,
           act_ref, filt_ref, bias_ref, gout_ref, load_sem, acts, gate, gout, gate_k, w_fwd, w_flip, w_bwd, part, part_in, pack, pack_in, total,
           a_send, a_recv, h_send, h_recv, p_send, p_recv, g_send, g_recv, q_send, q_recv, r_sem, t_sem):
    n_gx, n_gy, px, py, nz, ch, rows, n_red, factor = sizes
    cin = 2 * ch
    inner = py * nz
    gx, gy, af = lax.axis_index("gx"), lax.axis_index("gy"), lax.axis_index("af")
    other = 1 - af
    group = n_gx * n_gy
    me = gx * n_gy + gy

    loads = [pltpu.make_async_copy(src, dst, load_sem.at[at]) for at, (src, dst) in enumerate((
        (act_hbm, act_ref), (filt_hbm, filt_ref), (bias_hbm, bias_ref), (gout_hbm, gout_ref)))]
    for load in loads:
        load.start()

    for field in (acts, gate):
        for at in (0, px + 1):
            field[at] = jnp.zeros(field.shape[1:], BF16)
        for at in (0, nz + inner):
            field[1:px + 1, ..., at:at + nz] = jnp.zeros((px, *field.shape[1:-1], nz), BF16)

    barrier = pltpu.get_barrier_semaphore()
    everyone = 2 * group

    def greet(t, _):
        peer = lax.rem(me * 2 + af + t, everyone)
        pl.semaphore_signal(
            barrier, inc=1,
            device_id=(peer // (2 * n_gy), lax.rem(peer // 2, n_gy), lax.rem(peer, 2)),
            device_id_type=MESH)
        return 0

    lax.fori_loop(1, everyone, greet, 0)
    loads[0].wait()
    for xo in range(px):
        acts[xo + 1, pl.ds(af, 1), :, nz:nz + inner] = (
            act_ref[:, xo].reshape(1, ch, inner))
    pl.semaphore_wait(barrier, everyone - 1)

    def spans(d):
        dx, dy = d
        sx = {1: (px, 1), -1: (1, 1), 0: (1, px)}[dx]
        tx = {1: (0, 1), -1: (px + 1, 1), 0: (1, px)}[dx]
        sy = {1: (py, 1), -1: (1, 1), 0: (1, py)}[dy]
        ty = {1: (0, 1), -1: (py + 1, 1), 0: (1, py)}[dy]
        lanes = lambda s: pl.ds(s[0] * nz, s[1] * nz)
        return (pl.ds(*sx), lanes(sy)), (pl.ds(*tx), lanes(ty))

    def there(d):
        return (gx + d[0] >= 0) & (gx + d[0] < n_gx) & (gy + d[1] >= 0) & (gy + d[1] < n_gy)

    def back(d):
        return there((-d[0], -d[1]))

    def act_copy(s):
        d = SIDES[s]
        (sx, sl), (tx, tl) = spans(d)
        return pltpu.make_async_remote_copy(
            src_ref=acts.at[sx, af, :, sl], dst_ref=acts.at[tx, af, :, tl],
            send_sem=a_send.at[s], recv_sem=a_recv.at[s],
            device_id=(gx + d[0], gy + d[1], af), device_id_type=MESH)

    def hand_on(s, which):
        tx, tl = spans(SIDES[s])[1]
        block = acts.at[tx, which, :, tl]
        return pltpu.make_async_remote_copy(
            src_ref=block, dst_ref=block, send_sem=h_send.at[s], recv_sem=h_recv.at[s],
            device_id=(gx, gy, other), device_id_type=MESH)

    def gate_copy(s):
        d = SIDES[s]
        (sx, sl), (tx, tl) = spans(d)
        return pltpu.make_async_remote_copy(
            src_ref=gate.at[sx, :, sl], dst_ref=gate.at[tx, :, tl],
            send_sem=g_send.at[s], recv_sem=g_recv.at[s],
            device_id=(gx + d[0], gy + d[1], af), device_id_type=MESH)

    def partner_copy(which):
        block = acts.at[pl.ds(1, px), which, :, pl.ds(nz, inner)]
        return pltpu.make_async_remote_copy(
            src_ref=block, dst_ref=block, send_sem=p_send, recv_sem=p_recv,
            device_id=(gx, gy, other), device_id_type=MESH)

    order = sorted(range(8), key=lambda s: SIDES[s][1] != 0)
    arrival = sorted(range(8), key=lambda s: 2 * (SIDES[s][0] != 0) + (SIDES[s][1] != 0))
    for s in order:
        @pl.when(there(SIDES[s]))
        def _():
            act_copy(s).start()
    partner_copy(af).start()

    for load in loads[1:]:
        load.wait()
    for xo in range(px):
        gout[xo] = gout_ref[:, xo].reshape(ch, inner)
    for i in range(3):
        for j in range(3):
            tap = filt_ref[i, j * 3 * ch:(j + 1) * 3 * ch, :]
            w_fwd[j, :, i * cin:(i + 1) * cin] = tap
            for k in range(3):
                w_flip[j, (2 - i) * ch:(3 - i) * ch, k * cin:(k + 1) * cin] = (
                    tap[k * ch:(k + 1) * ch, :])
    for j in range(3):
        w_bwd[j] = w_flip[j].astype(F32).T.astype(BF16)
    eye = (lax.broadcasted_iota(jnp.int32, (ch, ch), 0)
           == lax.broadcasted_iota(jnp.int32, (ch, ch), 1))
    bias = jnp.sum(jnp.where(eye, bias_ref[...], 0.0), axis=1, keepdims=True)

    for s in arrival:
        @pl.when(back(SIDES[s]))
        def _():
            act_copy(s).wait_recv()
            hand_on(s, af).start()
    partner_copy(other).wait_recv()
    for s in arrival:
        @pl.when(back(SIDES[s]))
        def _():
            hand_on(s, other).wait_recv()

    lane = lax.broadcasted_iota(jnp.int32, (1, nz), 1)

    def from_below(v):
        return jnp.where(lane == 0, 0.0, pltpu.roll(v, 1, 1))

    def from_above(v):
        return jnp.where(lane == nz - 1, 0.0, pltpu.roll(v, nz - 1, 1))

    step = 2 if py % 2 == 0 else 1
    bias_sum = jnp.zeros((ch, nz), F32)
    for xo in range(px):
        for y0 in range(0, py, step):
            acc = None
            for j in range(3):
                window = acts[xo:xo + 3, :, :, (y0 + j) * nz:(y0 + j + step) * nz]
                term = jnp.dot(w_fwd[j], window.reshape(3 * cin, step * nz),
                               preferred_element_type=F32)
                acc = term if acc is None else acc + term
            for u in range(step):
                cut = acc[:, u * nz:(u + 1) * nz]
                pre = (cut[ch:2 * ch] + from_below(cut[:ch]) + from_above(cut[2 * ch:])) + bias
                lanes = slice((y0 + u) * nz, (y0 + u + 1) * nz)
                squash = 1.0 / (1.0 + jnp.exp(-pre))
                g = gout[xo, :, lanes].astype(F32) * squash * (1.0 + pre * (1.0 - squash))
                rounded = g.astype(BF16)
                g = rounded.astype(F32)
                bias_sum = bias_sum + g
                gate[xo + 1, :, (y0 + u + 1) * nz:(y0 + u + 2) * nz] = rounded
                gate_k[xo, 0:ch, lanes] = from_above(g).astype(BF16)
                gate_k[xo, ch:2 * ch, lanes] = rounded
                gate_k[xo, 2 * ch:3 * ch, lanes] = from_below(g).astype(BF16)

    head = ch
    main, fold = 3 * ch, 3 * ch // 2
    whole = jnp.sum(bias_sum, axis=1, keepdims=True) * factor + jnp.zeros((ch, 2 * cin), F32)
    wide = lax.broadcasted_iota(jnp.int32, (1, 2 * cin), 1)

    def two_parts(v):
        high = v.astype(BF16).astype(F32)
        return jnp.where(wide < cin, high, v - high)

    pack[0:head, :] = two_parts(whole).astype(BF16)
    used = head + 3 * (main + fold)
    if n_red * rows > used:
        pack[used:n_red * rows, :] = jnp.zeros((n_red * rows - used, 2 * cin), BF16)

    def scatter(first, count):
        def body(t, _):
            peer = first + lax.rem(me + t, count)

            @pl.when(peer != me)
            def _():
                slot = lax.rem(peer - me + group, group) - 1
                pltpu.make_async_remote_copy(
                    src_ref=pack.at[pl.ds(peer * rows, rows)],
                    dst_ref=pack_in.at[pl.ds(slot * rows, rows)],
                    send_sem=r_sem.at[0], recv_sem=r_sem.at[1],
                    device_id=(peer // n_gy, lax.rem(peer, n_gy), af), device_id_type=MESH).start()
            return 0

        lax.fori_loop(0, count, body, 0)

    ready = 0
    for j in range(3):
        acc = None
        for xo in range(px):
            window = acts[xo:xo + 3, :, :, j * nz:j * nz + inner].reshape(3 * cin, inner)
            term = lax.dot_general(gate_k[xo], window, (((1,), (1,)), ((), ())),
                                   preferred_element_type=F32)
            acc = term if acc is None else acc + term
        acc = (acc * factor).astype(BF16)
        base = head + j * (main + fold)
        pack[base:base + main, :] = acc[:, :2 * cin]
        pack[base + main:base + main + fold, 0:cin] = acc[:fold, 2 * cin:]
        pack[base + main:base + main + fold, cin:2 * cin] = acc[fold:, 2 * cin:]
        done = n_red if j == 2 else (base + main + fold) // rows
        if done > ready:
            scatter(ready, done - ready)
        ready = done

    for s in order:
        @pl.when(there(SIDES[s]))
        def _():
            gate_copy(s).start()

    def peer_of(t):
        return lax.rem(me + t, group)

    def settle(ref, count, sem):
        block = ref.at[pl.ds(0, count * rows)]
        return pltpu.make_async_copy(block, block, sem)

    @pl.when(me < n_red)
    def _():
        settle(pack_in, group - 1, r_sem.at[1]).wait()
        here = pl.multiple_of(me * rows, 16)
        summed = pack[pl.ds(here, rows), :].astype(F32)

        def add(t, v):
            return v + pack_in[pl.ds(pl.multiple_of(t * rows, 16), rows), :].astype(F32)

        if group <= 32:
            for t in range(group - 1):
                summed = add(t, summed)
        else:
            summed = lax.fori_loop(0, group - 1, add, summed)
        both = two_parts(summed + pltpu.roll(summed, cin, 1))
        at = here + lax.broadcasted_iota(jnp.int32, (rows, 1), 0)
        total[pl.ds(here, rows), :] = jnp.where(at < head, both, summed).astype(BF16)

        def share(t, _):
            peer = peer_of(t)
            mine = total.at[pl.ds(here, rows)]
            pltpu.make_async_remote_copy(
                src_ref=mine, dst_ref=mine, send_sem=t_sem.at[0], recv_sem=t_sem.at[1],
                device_id=(peer // n_gy, lax.rem(peer, n_gy), af), device_id_type=MESH).start()
            return 0

        lax.fori_loop(1, group, share, 0)

    for s in order:
        @pl.when(back(SIDES[s]))
        def _():
            gate_copy(s).wait_recv()

    def part_copy(xo):
        return pltpu.make_async_remote_copy(
            src_ref=part.at[xo, other], dst_ref=part_in.at[xo],
            send_sem=q_send.at[xo], recv_sem=q_recv.at[xo],
            device_id=(gx, gy, other), device_id_type=MESH)

    for xo in range(px):
        for y0 in range(0, py, step):
            acc = None
            for j in range(3):
                at = y0 + 2 - j
                window = gate[xo:xo + 3, :, at * nz:(at + step) * nz].reshape(3 * ch, step * nz)
                term = jnp.dot(w_bwd[j], window, preferred_element_type=F32)
                acc = term if acc is None else acc + term
            for u in range(step):
                cut = acc[:, u * nz:(u + 1) * nz]
                full = (cut[cin:2 * cin] + from_above(cut[:cin]) + from_below(cut[2 * cin:]))
                part[xo, :, :, (y0 + u) * nz:(y0 + u + 1) * nz] = full.reshape(2, ch, nz)
        part_copy(xo).start()

    for xo in range(px):
        part_copy(xo).wait_recv()
        mine = part[xo, pl.ds(af, 1), :, :].reshape(ch, inner)
        igrad_ref[:, xo] = (mine + part_in[xo]).reshape(ch, py, nz).astype(BF16)

    for s in order:
        @pl.when(there(SIDES[s]))
        def _():
            act_copy(s).wait_send()
            gate_copy(s).wait_send()

        @pl.when(back(SIDES[s]))
        def _():
            hand_on(s, af).wait_send()
    partner_copy(af).wait_send()
    for xo in range(px):
        part_copy(xo).wait_send()

    @pl.when(me < n_red)
    def _():
        settle(pack, n_red - 1, r_sem.at[0]).wait()
        settle(pack_in, group - 1, t_sem.at[0]).wait()
        settle(total, n_red - 1, t_sem.at[1]).wait()

    if n_red < group:
        @pl.when(me >= n_red)
        def _():
            settle(pack, n_red, r_sem.at[0]).wait()
            settle(total, n_red, t_sem.at[1]).wait()
    fgrad_ref[...] = total[...]


def unpack(sizes, igrad_ref, packed, igrad_out, fgrad_out, bias_out, taps, bias, sems):
    ch, cin = sizes
    early = pltpu.make_async_copy(igrad_ref, igrad_out, sems.at[0])
    early.start()
    head, main, fold = ch, 3 * ch, 3 * ch // 2
    column = (packed[0:head, :].astype(F32) + pltpu.roll(packed[0:head, :].astype(F32), cin, 1))[:, :1]
    eye = (lax.broadcasted_iota(jnp.int32, (ch, ch), 0)
           == lax.broadcasted_iota(jnp.int32, (ch, ch), 1))
    bias[...] = jnp.sum(jnp.where(eye, column, 0.0), axis=0, keepdims=True)
    small = pltpu.make_async_copy(bias, bias_out, sems.at[1])
    small.start()
    for j in range(3):
        base = head + j * (main + fold)
        block = packed[base:base + main + fold, :].astype(F32)
        at = j * main
        taps[0, at:at + main, :] = block[:main, :cin]
        taps[1, at:at + main, :] = block[:main, cin:]
        taps[2, at:at + fold, :] = block[main:, :cin]
        taps[2, at + fold:at + main, :] = block[main:, cin:]
    large = pltpu.make_async_copy(taps, fgrad_out, sems.at[2])
    large.start()
    early.wait()
    small.wait()
    large.wait()


def per_device(activations, filters, conv_bias, grad_output):
    ch, px, py, nz = activations.shape
    n_gx, n_gy = lax.axis_size("gx"), lax.axis_size("gy")
    group = n_gx * n_gy
    cin = 2 * ch
    inner = py * nz
    factor = 1.0 / math.sqrt(px * n_gx * py * n_gy * nz)
    used = ch + 3 * (3 * ch + 3 * ch // 2)
    rows = 16 * (-(-(used // 16) // group))
    n_red = -(-used // rows)

    vmem = pl.BlockSpec(memory_space=pltpu.VMEM)
    hbm = pl.BlockSpec(memory_space=pltpu.HBM)
    dma = pltpu.SemaphoreType.DMA
    igrad, packed = pl.pallas_call(
        functools.partial(kernel, (n_gx, n_gy, px, py, nz, ch, rows, n_red, factor)),
        out_shape=(jax.ShapeDtypeStruct((ch, px, py, nz), BF16),
                   jax.ShapeDtypeStruct((n_red * rows, 2 * cin), BF16)),
        in_specs=[hbm] * 4,
        out_specs=(vmem, vmem),
        scratch_shapes=[
            pltpu.VMEM((ch, px, py, nz), BF16),
            pltpu.VMEM((3, 9 * ch, cin), BF16),
            pltpu.VMEM((1, ch), F32),
            pltpu.VMEM((ch, px, py, nz), BF16),
            dma((4,)),
            pltpu.VMEM((px + 2, 2, ch, (py + 2) * nz), BF16),
            pltpu.VMEM((px + 2, ch, (py + 2) * nz), BF16),
            pltpu.VMEM((px, ch, inner), BF16),
            pltpu.VMEM((px, 3 * ch, inner), BF16),
            pltpu.VMEM((3, 3 * ch, 3 * cin), BF16),
            pltpu.VMEM((3, 3 * ch, 3 * cin), BF16),
            pltpu.VMEM((3, 3 * cin, 3 * ch), BF16),
            pltpu.VMEM((px, 2, ch, inner), F32),
            pltpu.VMEM((px, ch, inner), F32),
            pltpu.VMEM((n_red * rows, 2 * cin), BF16),
            pltpu.VMEM(((group - 1) * rows, 2 * cin), BF16),
            pltpu.VMEM((n_red * rows, 2 * cin), BF16),
            dma((8,)), dma((8,)), dma((8,)), dma((8,)), dma, dma, dma((8,)), dma((8,)),
            dma((px,)), dma((px,)), dma((2,)), dma((2,)),
        ],
        compiler_params=pltpu.CompilerParams(
            collective_id=0, has_side_effects=True, vmem_limit_bytes=24 * 1024 * 1024),
    )(*[pltpu.with_memory_space_constraint(v, pltpu.HBM) for v in (activations, filters.reshape(3, 9 * ch, cin), conv_bias.reshape(1, ch), grad_output)])
    input_grads, filter_grads, bias_grads = pl.pallas_call(
        functools.partial(unpack, (ch, cin)),
        out_shape=(jax.ShapeDtypeStruct(activations.shape, BF16),
                   jax.ShapeDtypeStruct((3, 9 * ch, cin), F32),
                   jax.ShapeDtypeStruct((1, ch), F32)),
        in_specs=[vmem] * 2,
        out_specs=(hbm,) * 3,
        scratch_shapes=[pltpu.VMEM((3, 9 * ch, cin), F32), pltpu.VMEM((1, ch), F32), dma((3,))],
        compiler_params=pltpu.CompilerParams(vmem_limit_bytes=8 * 1024 * 1024),
    )(igrad, packed)
    return (input_grads, filter_grads.reshape(filters.shape), bias_grads.reshape(ch))


def solution(mesh):
    return jax.shard_map(
        per_device,
        mesh=mesh,
        in_specs=(
            P("af", "gx", "gy", None),
            P(None, None, None, "af", None),
            P("af"),
            P("af", "gx", "gy", None),
        ),
        out_specs=(P("af", "gx", "gy", None), P(None, None, None, "af", None), P("af")),
        check_vma=False,
    )
```

profile of v0, /device:TPU:0, one launch (start us, length us, event | category | flops | bytes accessed | tf_op | source)
XLA Modules:
  0.0 26.3 jit_solution(9399384602560466830)
XLA Ops:
  0.6 24.7 %shard_map.67 = (bf16[32,2,8,128]{3,2,1,0:T(8,128)(2,1)S(1)}, bf16[480,128]{1,0:T(8,128)(2,1)S(1)}) custom-call(bf16[32,2,8,128]{3,2,1,0:T(8,128)(2,1)} %act_hbm.1, bf16[3,288,64]{2,1,0:T(8,128)(2,1)} %bitcast.4, f32[1,32]{1,0:T(1,128)} %bitcast.5, bf16[32,2,8,128]{3,2,1,0:T(8,128)(2,1)} %gout_hbm.1), custom_call_target="tpu_custom_call" | custom-call | tf_op jit(solution)/shard_map/pallas_call | solution.py:353
  25.4 0.9 %shard_map.68 = (bf16[32,2,8,128]{3,2,1,0:T(8,128)(2,1)}, f32[3,288,64]{2,1,0:T(8,128)}, f32[1,32]{1,0:T(1,128)}) custom-call(bf16[32,2,8,128]{3,2,1,0:T(8,128)(2,1)S(1)} %get-tuple-element.8.igrad_ref, bf16[480,128]{1,0:T(8,128)(2,1)S(1)} %get-tuple-element.9.packed), custom_call_target="tpu_custom_call" | custom-call | tf_op jit(solution)/shard_map/pallas_call | solution.py:383
where the time goes:
time: 26.5 us; the launch traced here: 26.3 us
  Pallas kernels  25.7 us (97%)
  between operations  0.64 us (2%)
    pallas_call x1, Pallas kernels, per_device(): pl.pallas_call(functools.partial(kernel, (n_gx, n_gy, px, py, nz, ch, row...  24.7 us
    pallas_call x1, Pallas kernels, per_device(): pl.pallas_call(functools.partial(unpack, (ch, cin)), out_shape=(jax.Shape...  0.95 us

commit v1 on v0

--- a/solution.py
+++ b/solution.py
@@ -14,8 +14,8 @@
 
 
 def kernel(sizes, act_hbm, filt_hbm, bias_hbm, gout_hbm, igrad_ref, fgrad_ref,
-           act_ref, filt_ref, bias_ref, gout_ref, load_sem, acts, gate, gout, gate_k, w_fwd, w_flip, w_bwd, part, part_in, pack, pack_in, total,
-           a_send, a_recv, h_send, h_recv, p_send, p_recv, g_send, g_recv, q_send, q_recv, r_sem, t_sem):
+           act_ref, filt_ref, bias_ref, gout_ref, load_sem, acts, gate, gout, gate_k, w_fwd, w_flip, w_bwd, part, part_in, pack, pack_in, mine, total,
+           a_send, a_recv, h_send, h_recv, p_send, p_recv, g_send, g_recv, q_send, q_recv, r_sem, t_sem, near):
     n_gx, n_gy, px, py, nz, ch, rows, n_red, factor = sizes
     cin = 2 * ch
     inner = py * nz
@@ -23,35 +23,38 @@
     other = 1 - af
     group = n_gx * n_gy
     me = gx * n_gy + gy
+    rounds = max(n_gx, n_gy) - 2
 
     loads = [pltpu.make_async_copy(src, dst, load_sem.at[at]) for at, (src, dst) in enumerate((
         (act_hbm, act_ref), (filt_hbm, filt_ref), (bias_hbm, bias_ref), (gout_hbm, gout_ref)))]
     for load in loads:
         load.start()
 
-    for field in (acts, gate):
-        for at in (0, px + 1):
-            field[at] = jnp.zeros(field.shape[1:], BF16)
-        for at in (0, nz + inner):
-            field[1:px + 1, ..., at:at + nz] = jnp.zeros((px, *field.shape[1:-1], nz), BF16)
+    def there(d):
+        return (gx + d[0] >= 0) & (gx + d[0] < n_gx) & (gy + d[1] >= 0) & (gy + d[1] < n_gy)
+
+    def back(d):
+        return there((-d[0], -d[1]))
 
     barrier = pltpu.get_barrier_semaphore()
-    everyone = 2 * group
-
-    def greet(t, _):
-        peer = lax.rem(me * 2 + af + t, everyone)
-        pl.semaphore_signal(
-            barrier, inc=1,
-            device_id=(peer // (2 * n_gy), lax.rem(peer // 2, n_gy), lax.rem(peer, 2)),
-            device_id_type=MESH)
-        return 0
-
-    lax.fori_loop(1, everyone, greet, 0)
-    loads[0].wait()
-    for xo in range(px):
-        acts[xo + 1, pl.ds(af, 1), :, nz:nz + inner] = (
-            act_ref[:, xo].reshape(1, ch, inner))
-    pl.semaphore_wait(barrier, everyone - 1)
+    around = sum(there(d).astype(jnp.int32) for d in SIDES)
+    for d in SIDES:
+        @pl.when(there(d))
+        def _():
+            for core in range(2):
+                pl.semaphore_signal(
+                    barrier, inc=1, device_id=(gx + d[0], gy + d[1], core), device_id_type=MESH)
+    pl.semaphore_signal(barrier, inc=1, device_id=(gx, gy, other), device_id_type=MESH)
+
+    def tell(at):
+        for d in SIDES:
+            @pl.when(there(d))
+            def _():
+                pl.semaphore_signal(
+                    near.at[at], inc=1, device_id=(gx + d[0], gy + d[1], af), device_id_type=MESH)
+
+    def hear(at):
+        pl.semaphore_wait(near.at[at], around)
 
     def spans(d):
         dx, dy = d
@@ -62,26 +65,43 @@
         lanes = lambda s: pl.ds(s[0] * nz, s[1] * nz)
         return (pl.ds(*sx), lanes(sy)), (pl.ds(*tx), lanes(ty))
 
-    def there(d):
-        return (gx + d[0] >= 0) & (gx + d[0] < n_gx) & (gy + d[1] >= 0) & (gy + d[1] < n_gy)
-
-    def back(d):
-        return there((-d[0], -d[1]))
-
-    def act_copy(s):
+    for d in SIDES:
+        tx, tl = spans(d)[1]
+        missing = ~back(d)
+
+        @pl.when(missing)
+        def _():
+            gate[tx, :, tl] = jnp.zeros((tx.size, ch, tl.size), BF16)
+
+        if d[0] != 0 and d[1] != 0:
+            missing &= (af == 1) | ~back((d[0], 0))
+
+        @pl.when(missing)
+        def _():
+            acts[tx, :, :, tl] = jnp.zeros((tx.size, 2, ch, tl.size), BF16)
+
+    loads[0].wait()
+    for xo in range(px):
+        acts[xo + 1, pl.ds(af, 1), :, nz:nz + inner] = (
+            act_ref[:, xo].reshape(1, ch, inner))
+    pl.semaphore_wait(barrier, 2 * around + 1)
+
+    def act_copy(s, half, core):
         d = SIDES[s]
         (sx, sl), (tx, tl) = spans(d)
         return pltpu.make_async_remote_copy(
-            src_ref=acts.at[sx, af, :, sl], dst_ref=acts.at[tx, af, :, tl],
-            send_sem=a_send.at[s], recv_sem=a_recv.at[s],
-            device_id=(gx + d[0], gy + d[1], af), device_id_type=MESH)
-
-    def hand_on(s, which):
-        tx, tl = spans(SIDES[s])[1]
-        block = acts.at[tx, which, :, tl]
+            src_ref=acts.at[sx, half, :, sl], dst_ref=acts.at[tx, half, :, tl],
+            send_sem=a_send.at[2 * s + core], recv_sem=a_recv.at[2 * s + half],
+            device_id=(gx + d[0], gy + d[1], core), device_id_type=MESH)
+
+    def cores(s):
+        return (1,) if SIDES[s][0] != 0 else (1, 0)
+
+    def hand_on(at):
+        plane = acts.at[pl.ds((0, px + 1)[at], 1)]
         return pltpu.make_async_remote_copy(
-            src_ref=block, dst_ref=block, send_sem=h_send.at[s], recv_sem=h_recv.at[s],
-            device_id=(gx, gy, other), device_id_type=MESH)
+            src_ref=plane, dst_ref=plane, send_sem=h_send.at[at], recv_sem=h_recv.at[at],
+            device_id=(gx, gy, 0), device_id_type=MESH)
 
     def gate_copy(s):
         d = SIDES[s]
@@ -98,12 +118,14 @@
             device_id=(gx, gy, other), device_id_type=MESH)
 
     order = sorted(range(8), key=lambda s: SIDES[s][1] != 0)
-    arrival = sorted(range(8), key=lambda s: 2 * (SIDES[s][0] != 0) + (SIDES[s][1] != 0))
     for s in order:
         @pl.when(there(SIDES[s]))
         def _():
-            act_copy(s).start()
+            for core in cores(s):
+                act_copy(s, af, core).start()
     partner_copy(af).start()
+    if rounds > 0:
+        tell(0)
 
     for load in loads[1:]:
         load.wait()
@@ -122,16 +144,31 @@
            == lax.broadcasted_iota(jnp.int32, (ch, ch), 1))
     bias = jnp.sum(jnp.where(eye, bias_ref[...], 0.0), axis=1, keepdims=True)
 
-    for s in arrival:
-        @pl.when(back(SIDES[s]))
-        def _():
-            act_copy(s).wait_recv()
-            hand_on(s, af).start()
+    for at in range(1, rounds):
+        hear(at - 1)
+        tell(at)
+
+    for at, dx in enumerate((1, -1)):
+        @pl.when((af == 1) & back((dx, 0)))
+        def _():
+            for s in order:
+                if SIDES[s][0] == dx:
+                    @pl.when(back(SIDES[s]))
+                    def _():
+                        for half in range(2):
+                            act_copy(s, half, 1).wait_recv()
+            hand_on(at).start()
     partner_copy(other).wait_recv()
-    for s in arrival:
-        @pl.when(back(SIDES[s]))
-        def _():
-            hand_on(s, other).wait_recv()
+    for s in order:
+        if SIDES[s][0] == 0:
+            @pl.when(back(SIDES[s]))
+            def _():
+                for half in range(2):
+                    act_copy(s, half, 0).wait_recv()
+    for at, dx in enumerate((1, -1)):
+        @pl.when((af == 0) & back((dx, 0)))
+        def _():
+            hand_on(at).wait_recv()
 
     lane = lax.broadcasted_iota(jnp.int32, (1, nz), 1)
 
@@ -180,20 +217,21 @@
         pack[used:n_red * rows, :] = jnp.zeros((n_red * rows - used, 2 * cin), BF16)
 
     def scatter(first, count):
-        def body(t, _):
-            peer = first + lax.rem(me + t, count)
-
-            @pl.when(peer != me)
+        for b in range(first, first + count):
+            chip = 2 * b + af
+            own = (af == 1) & (chip == me)
+            block = pack.at[pl.ds(b * rows, rows)]
+            slot = pack_in.at[pl.ds(pl.multiple_of(me * rows, 16), rows)]
+
+            @pl.when(own)
             def _():
-                slot = lax.rem(peer - me + group, group) - 1
+                pltpu.make_async_copy(block, slot, r_sem.at[1]).start()
+
+            @pl.when(~own)
+            def _():
                 pltpu.make_async_remote_copy(
-                    src_ref=pack.at[pl.ds(peer * rows, rows)],
-                    dst_ref=pack_in.at[pl.ds(slot * rows, rows)],
-                    send_sem=r_sem.at[0], recv_sem=r_sem.at[1],
-                    device_id=(peer // n_gy, lax.rem(peer, n_gy), af), device_id_type=MESH).start()
-            return 0
-
-        lax.fori_loop(0, count, body, 0)
+                    src_ref=block, dst_ref=slot, send_sem=r_sem.at[0], recv_sem=r_sem.at[1],
+                    device_id=(chip // n_gy, lax.rem(chip, n_gy), 1), device_id_type=MESH).start()
 
     ready = 0
     for j in range(3):
@@ -209,6 +247,8 @@
         pack[base + main:base + main + fold, 0:cin] = acc[:fold, 2 * cin:]
         pack[base + main:base + main + fold, cin:2 * cin] = acc[fold:, 2 * cin:]
         done = n_red if j == 2 else (base + main + fold) // rows
+        if j == 0 and rounds > 0:
+            hear(rounds - 1)
         if done > ready:
             scatter(ready, done - ready)
         ready = done
@@ -218,40 +258,49 @@
         def _():
             gate_copy(s).start()
 
-    def peer_of(t):
-        return lax.rem(me + t, group)
-
     def settle(ref, count, sem):
         block = ref.at[pl.ds(0, count * rows)]
         return pltpu.make_async_copy(block, block, sem)
 
-    @pl.when(me < n_red)
+    half, at_block = lax.rem(me, 2), me // 2
+    reducer = (af == 1) & (me < 2 * n_red)
+    here = pl.multiple_of(at_block * rows, 16)
+
+    def share(peer):
+        own = (half == 1) & (peer == me)
+        place = total.at[pl.ds(here, rows)]
+
+        @pl.when(own)
+        def _():
+            pltpu.make_async_copy(mine, place, t_sem.at[1]).start()
+
+        @pl.when(~own)
+        def _():
+            pltpu.make_async_remote_copy(
+                src_ref=mine, dst_ref=place, send_sem=t_sem.at[0], recv_sem=t_sem.at[1],
+                device_id=(peer // n_gy, peer % n_gy, half), device_id_type=MESH).start()
+
+    @pl.when(reducer)
     def _():
-        settle(pack_in, group - 1, r_sem.at[1]).wait()
-        here = pl.multiple_of(me * rows, 16)
-        summed = pack[pl.ds(here, rows), :].astype(F32)
+        settle(pack_in, group, r_sem.at[1]).wait()
 
         def add(t, v):
             return v + pack_in[pl.ds(pl.multiple_of(t * rows, 16), rows), :].astype(F32)
 
+        summed = pack_in[0:rows, :].astype(F32)
         if group <= 32:
-            for t in range(group - 1):
+            for t in range(1, group):
                 summed = add(t, summed)
         else:
-            summed = lax.fori_loop(0, group - 1, add, summed)
+            summed = lax.fori_loop(1, group, add, summed)
         both = two_parts(summed + pltpu.roll(summed, cin, 1))
         at = here + lax.broadcasted_iota(jnp.int32, (rows, 1), 0)
-        total[pl.ds(here, rows), :] = jnp.where(at < head, both, summed).astype(BF16)
-
-        def share(t, _):
-            peer = peer_of(t)
-            mine = total.at[pl.ds(here, rows)]
-            pltpu.make_async_remote_copy(
-                src_ref=mine, dst_ref=mine, send_sem=t_sem.at[0], recv_sem=t_sem.at[1],
-                device_id=(peer // n_gy, lax.rem(peer, n_gy), af), device_id_type=MESH).start()
-            return 0
-
-        lax.fori_loop(1, group, share, 0)
+        mine[...] = jnp.where(at < head, both, summed).astype(BF16)
+        if group <= 32:
+            for peer in range(group):
+                share(peer)
+        else:
+            lax.fori_loop(0, group, lambda peer, _: share(peer) or 0, 0)
 
     for s in order:
         @pl.when(back(SIDES[s]))
@@ -286,27 +335,33 @@
     for s in order:
         @pl.when(there(SIDES[s]))
         def _():
-            act_copy(s).wait_send()
+            for core in cores(s):
+                act_copy(s, af, core).wait_send()
             gate_copy(s).wait_send()
-
-        @pl.when(back(SIDES[s]))
-        def _():
-            hand_on(s, af).wait_send()
+    for at, dx in enumerate((1, -1)):
+        @pl.when((af == 1) & back((dx, 0)))
+        def _():
+            hand_on(at).wait_send()
     partner_copy(af).wait_send()
     for xo in range(px):
         part_copy(xo).wait_send()
 
-    @pl.when(me < n_red)
+    kept = reducer & (half == 1)
+
+    @pl.when(kept)
     def _():
         settle(pack, n_red - 1, r_sem.at[0]).wait()
         settle(pack_in, group - 1, t_sem.at[0]).wait()
-        settle(total, n_red - 1, t_sem.at[1]).wait()
-
-    if n_red < group:
-        @pl.when(me >= n_red)
-        def _():
-            settle(pack, n_red, r_sem.at[0]).wait()
-            settle(total, n_red, t_sem.at[1]).wait()
+
+    @pl.when(~kept)
+    def _():
+        settle(pack, n_red, r_sem.at[0]).wait()
+
+    @pl.when(reducer & (half == 0))
+    def _():
+        settle(pack_in, group, t_sem.at[0]).wait()
+
+    settle(total, n_red, t_sem.at[1]).wait()
     fgrad_ref[...] = total[...]
 
 
@@ -344,7 +399,7 @@
     inner = py * nz
     factor = 1.0 / math.sqrt(px * n_gx * py * n_gy * nz)
     used = ch + 3 * (3 * ch + 3 * ch // 2)
-    rows = 16 * (-(-(used // 16) // group))
+    rows = 16 * (-(-(used // 16) // (group // 2)))
     n_red = -(-used // rows)
 
     vmem = pl.BlockSpec(memory_space=pltpu.VMEM)
@@ -372,10 +427,12 @@
             pltpu.VMEM((px, 2, ch, inner), F32),
             pltpu.VMEM((px, ch, inner), F32),
             pltpu.VMEM((n_red * rows, 2 * cin), BF16),
-            pltpu.VMEM(((group - 1) * rows, 2 * cin), BF16),
+            pltpu.VMEM((group * rows, 2 * cin), BF16),
+            pltpu.VMEM((rows, 2 * cin), BF16),
             pltpu.VMEM((n_red * rows, 2 * cin), BF16),
-            dma((8,)), dma((8,)), dma((8,)), dma((8,)), dma, dma, dma((8,)), dma((8,)),
+            dma((16,)), dma((16,)), dma((2,)), dma((2,)), dma, dma, dma((8,)), dma((8,)),
             dma((px,)), dma((px,)), dma((2,)), dma((2,)),
+            pltpu.SemaphoreType.REGULAR((max(1, max(n_gx, n_gy) - 2),)),
         ],
         compiler_params=pltpu.CompilerParams(
             collective_id=0, has_side_effects=True, vmem_limit_bytes=24 * 1024 * 1024),

time: 26.5 us -> 24.8 us (0.936)
  Pallas kernels: 25.7 us -> 24 us
    pallas_call x1, Pallas kernels: 24.7 us -> 23 us  [per_device(): pl.pallas_call(functools.partial(kernel, (n_gx, n_gy, px, py, nz, ch, row...]
where the time goes in v1:
time: 24.8 us; the launch traced here: 24.6 us
  Pallas kernels  24 us (97%)
  between operations  0.64 us (3%)
    pallas_call x1, Pallas kernels, per_device(): pl.pallas_call(functools.partial(kernel, (n_gx, n_gy, px, py, nz, ch, row...  23 us
    pallas_call x1, Pallas kernels, per_device(): pl.pallas_call(functools.partial(unpack, (ch, cin)), out_shape=(jax.Shape...  0.95 us

profile of v1, /device:TPU:0, one launch (start us, length us, event | category | flops | bytes accessed | tf_op | source)
XLA Modules:
  0.0 24.6 jit_solution(7263386289654598378)
XLA Ops:
  0.6 23.0 %shard_map.67 = (bf16[32,2,8,128]{3,2,1,0:T(8,128)(2,1)S(1)}, bf16[512,128]{1,0:T(8,128)(2,1)S(1)}) custom-call(bf16[32,2,8,128]{3,2,1,0:T(8,128)(2,1)} %act_hbm.1, bf16[3,288,64]{2,1,0:T(8,128)(2,1)} %bitcast.4, f32[1,32]{1,0:T(1,128)} %bitcast.5, bf16[32,2,8,128]{3,2,1,0:T(8,128)(2,1)} %gout_hbm.1), custom_call_target="tpu_custom_call" | custom-call | tf_op jit(solution)/shard_map/pallas_call | solution.py:408
  23.7 0.9 %shard_map.68 = (bf16[32,2,8,128]{3,2,1,0:T(8,128)(2,1)}, f32[3,288,64]{2,1,0:T(8,128)}, f32[1,32]{1,0:T(1,128)}) custom-call(bf16[32,2,8,128]{3,2,1,0:T(8,128)(2,1)S(1)} %get-tuple-element.8.igrad_ref, bf16[512,128]{1,0:T(8,128)(2,1)S(1)} %get-tuple-element.9.packed), custom_call_target="tpu_custom_call" | custom-call | tf_op jit(solution)/shard_map/pallas_call | solution.py:440

commit v2 on v1

--- a/solution.py
+++ b/solution.py
@@ -97,10 +97,10 @@
     def cores(s):
         return (1,) if SIDES[s][0] != 0 else (1, 0)
 
-    def hand_on(at):
-        plane = acts.at[pl.ds((0, px + 1)[at], 1)]
+    def hand_on(at, half):
+        plane = acts.at[pl.ds((0, px + 1)[at], 1), half]
         return pltpu.make_async_remote_copy(
-            src_ref=plane, dst_ref=plane, send_sem=h_send.at[at], recv_sem=h_recv.at[at],
+            src_ref=plane, dst_ref=plane, send_sem=h_send.at[2 * at + half], recv_sem=h_recv.at[2 * at + half],
             device_id=(gx, gy, 0), device_id_type=MESH)
 
     def gate_copy(s):
@@ -117,7 +117,7 @@
             src_ref=block, dst_ref=block, send_sem=p_send, recv_sem=p_recv,
             device_id=(gx, gy, other), device_id_type=MESH)
 
-    order = sorted(range(8), key=lambda s: SIDES[s][1] != 0)
+    order = sorted(range(8), key=lambda s: (SIDES[s][0] == 0) * 2 + (SIDES[s][1] == 0))
     for s in order:
         @pl.when(there(SIDES[s]))
         def _():
@@ -133,13 +133,7 @@
         gout[xo] = gout_ref[:, xo].reshape(ch, inner)
     for i in range(3):
         for j in range(3):
-            tap = filt_ref[i, j * 3 * ch:(j + 1) * 3 * ch, :]
-            w_fwd[j, :, i * cin:(i + 1) * cin] = tap
-            for k in range(3):
-                w_flip[j, (2 - i) * ch:(3 - i) * ch, k * cin:(k + 1) * cin] = (
-                    tap[k * ch:(k + 1) * ch, :])
-    for j in range(3):
-        w_bwd[j] = w_flip[j].astype(F32).T.astype(BF16)
+            w_fwd[j, :, i * cin:(i + 1) * cin] = filt_ref[i, j * 3 * ch:(j + 1) * 3 * ch, :]
     eye = (lax.broadcasted_iota(jnp.int32, (ch, ch), 0)
            == lax.broadcasted_iota(jnp.int32, (ch, ch), 1))
     bias = jnp.sum(jnp.where(eye, bias_ref[...], 0.0), axis=1, keepdims=True)
@@ -148,16 +142,16 @@
         hear(at - 1)
         tell(at)
 
-    for at, dx in enumerate((1, -1)):
-        @pl.when((af == 1) & back((dx, 0)))
-        def _():
-            for s in order:
-                if SIDES[s][0] == dx:
-                    @pl.when(back(SIDES[s]))
-                    def _():
-                        for half in range(2):
+    for half in (1, 0):
+        for at, dx in enumerate((1, -1)):
+            @pl.when((af == 1) & back((dx, 0)))
+            def _():
+                for s in order:
+                    if SIDES[s][0] == dx:
+                        @pl.when(back(SIDES[s]))
+                        def _():
                             act_copy(s, half, 1).wait_recv()
-            hand_on(at).start()
+                hand_on(at, half).start()
     partner_copy(other).wait_recv()
     for s in order:
         if SIDES[s][0] == 0:
@@ -168,7 +162,8 @@
     for at, dx in enumerate((1, -1)):
         @pl.when((af == 0) & back((dx, 0)))
         def _():
-            hand_on(at).wait_recv()
+            for half in range(2):
+                hand_on(at, half).wait_recv()
 
     lane = lax.broadcasted_iota(jnp.int32, (1, nz), 1)
 
@@ -216,9 +211,16 @@
     if n_red * rows > used:
         pack[used:n_red * rows, :] = jnp.zeros((n_red * rows - used, 2 * cin), BF16)
 
+    def way(chip):
+        at = chip // n_gy
+        return max(at, n_gx - 1 - at) + at
+
+    homes = sorted(range(0, group - 1, 2), key=lambda chip: (way(chip), -chip))[:n_red]
+    homes.sort(key=lambda chip: (-way(chip), chip))
+
     def scatter(first, count):
         for b in range(first, first + count):
-            chip = 2 * b + af
+            chip = homes[b] + af
             own = (af == 1) & (chip == me)
             block = pack.at[pl.ds(b * rows, rows)]
             slot = pack_in.at[pl.ds(pl.multiple_of(me * rows, 16), rows)]
@@ -258,12 +260,24 @@
         def _():
             gate_copy(s).start()
 
+    for i in range(3):
+        for j in range(3):
+            for k in range(3):
+                at = (3 * j + k) * ch
+                w_flip[j, (2 - i) * ch:(3 - i) * ch, k * cin:(k + 1) * cin] = filt_ref[i, at:at + ch, :]
+    for j in range(3):
+        w_bwd[j] = w_flip[j].astype(F32).T.astype(BF16)
+
     def settle(ref, count, sem):
         block = ref.at[pl.ds(0, count * rows)]
         return pltpu.make_async_copy(block, block, sem)
 
-    half, at_block = lax.rem(me, 2), me // 2
-    reducer = (af == 1) & (me < 2 * n_red)
+    half = lax.rem(me, 2)
+    at_block, found = jnp.int32(0), jnp.int32(0)
+    for b in range(n_red):
+        here = (me - half == homes[b]).astype(jnp.int32)
+        at_block, found = at_block + b * here, found + here
+    reducer = (af == 1) & (found > 0)
     here = pl.multiple_of(at_block * rows, 16)
 
     def share(peer):
@@ -341,7 +355,8 @@
     for at, dx in enumerate((1, -1)):
         @pl.when((af == 1) & back((dx, 0)))
         def _():
-            hand_on(at).wait_send()
+            for half in range(2):
+                hand_on(at, half).wait_send()
     partner_copy(af).wait_send()
     for xo in range(px):
         part_copy(xo).wait_send()
@@ -399,7 +414,7 @@
     inner = py * nz
     factor = 1.0 / math.sqrt(px * n_gx * py * n_gy * nz)
     used = ch + 3 * (3 * ch + 3 * ch // 2)
-    rows = 16 * (-(-(used // 16) // (group // 2)))
+    rows = 16 * (-(-(used // 16) // (group // 2 * 3 // 4)))
     n_red = -(-used // rows)
 
     vmem = pl.BlockSpec(memory_space=pltpu.VMEM)
@@ -430,7 +445,7 @@
             pltpu.VMEM((group * rows, 2 * cin), BF16),
             pltpu.VMEM((rows, 2 * cin), BF16),
             pltpu.VMEM((n_red * rows, 2 * cin), BF16),
-            dma((16,)), dma((16,)), dma((2,)), dma((2,)), dma, dma, dma((8,)), dma((8,)),
+            dma((16,)), dma((16,)), dma((4,)), dma((4,)), dma, dma, dma((8,)), dma((8,)),
             dma((px,)), dma((px,)), dma((2,)), dma((2,)),
             pltpu.SemaphoreType.REGULAR((max(1, max(n_gx, n_gy) - 2),)),
         ],

time: 24.8 us -> 23.3 us (0.940)
  Pallas kernels: 24 us -> 22.6 us
    pallas_call x1, Pallas kernels: 23 us -> 21.6 us  [per_device(): pl.pallas_call(functools.partial(kernel, (n_gx, n_gy, px, py, nz, ch, row...]
where the time goes in v2:
time: 23.3 us; the launch traced here: 23.2 us
  Pallas kernels  22.6 us (97%)
  between operations  0.64 us (3%)
    pallas_call x1, Pallas kernels, per_device(): pl.pallas_call(functools.partial(kernel, (n_gx, n_gy, px, py, nz, ch, row...  21.6 us
    pallas_call x1, Pallas kernels, per_device(): pl.pallas_call(functools.partial(unpack, (ch, cin)), out_shape=(jax.Shape...  0.95 us

profile of v2, /device:TPU:0, one launch (start us, length us, event | category | flops | bytes accessed | tf_op | source)
XLA Modules:
  0.0 23.2 jit_solution(6486435712783399647)
XLA Ops:
  0.6 21.6 %shard_map.67 = (bf16[32,2,8,128]{3,2,1,0:T(8,128)(2,1)S(1)}, bf16[480,128]{1,0:T(8,128)(2,1)S(1)}) custom-call(bf16[32,2,8,128]{3,2,1,0:T(8,128)(2,1)} %act_hbm.1, bf16[3,288,64]{2,1,0:T(8,128)(2,1)} %bitcast.4, f32[1,32]{1,0:T(1,128)} %bitcast.5, bf16[32,2,8,128]{3,2,1,0:T(8,128)(2,1)} %gout_hbm.1), custom_call_target="tpu_custom_call" | custom-call | tf_op jit(solution)/shard_map/pallas_call | solution.py:423
  22.2 0.9 %shard_map.68 = (bf16[32,2,8,128]{3,2,1,0:T(8,128)(2,1)}, f32[3,288,64]{2,1,0:T(8,128)}, f32[1,32]{1,0:T(1,128)}) custom-call(bf16[32,2,8,128]{3,2,1,0:T(8,128)(2,1)S(1)} %get-tuple-element.8.igrad_ref, bf16[480,128]{1,0:T(8,128)(2,1)S(1)} %get-tuple-element.9.packed), custom_call_target="tpu_custom_call" | custom-call | tf_op jit(solution)/shard_map/pallas_call | solution.py:455

commit v3 on v1

v3 whole, which is shorter than its diff:
```python
import functools
import math

import jax
import jax.numpy as jnp
from jax import lax
from jax.experimental import pallas as pl
from jax.experimental.pallas import tpu as pltpu
from jax.sharding import PartitionSpec as P

MESH = pl.DeviceIdType.MESH
F32, BF16 = jnp.float32, jnp.bfloat16
SIDES = [(dx, dy) for dx in (-1, 0, 1) for dy in (-1, 0, 1) if (dx, dy) != (0, 0)]


def kernel(sizes, act_hbm, filt_hbm, bias_hbm, gout_hbm, igrad_ref, fgrad_ref,
           act_ref, filt_ref, bias_ref, gout_ref, filt_in, bias_in, gout_in, load_sem, acts, gate, gout, gate_k, w_fwd, w_flip, w_bwd, part, ig_out, ig_in, pack, pack_in, mine, total,
           a_send, a_recv, c_send, c_recv, g_send, g_recv, q_send, q_recv, r_send, r_recv, t_send, t_recv, near):
    n_gx, n_gy, px, py, nz, ch, rows, n_red, factor = sizes
    cin = 2 * ch
    inner = py * nz
    gx, gy, af = lax.axis_index("gx"), lax.axis_index("gy"), lax.axis_index("af")
    other = 1 - af
    group = n_gx * n_gy
    me = gx * n_gy + gy
    rounds = max(n_gx, n_gy) - 2
    core0, core1 = af == 0, af == 1

    loads = [pltpu.make_async_copy(src, dst, load_sem.at[at]) for at, (src, dst) in enumerate((
        (act_hbm, act_ref), (filt_hbm, filt_ref), (bias_hbm, bias_ref), (gout_hbm, gout_ref)))]
    for load in loads:
        load.start()

    def there(d):
        return (gx + d[0] >= 0) & (gx + d[0] < n_gx) & (gy + d[1] >= 0) & (gy + d[1] < n_gy)

    def back(d):
        return there((-d[0], -d[1]))

    barrier = pltpu.get_barrier_semaphore()
    around = sum(there(d).astype(jnp.int32) for d in SIDES)
    for d in SIDES:
        @pl.when(there(d))
        def _():
            pl.semaphore_signal(
                barrier, inc=1, device_id=(gx + d[0], gy + d[1], 1), device_id_type=MESH)

        @pl.when(there(d) & core1)
        def _():
            pl.semaphore_signal(
                barrier, inc=1, device_id=(gx + d[0], gy + d[1], 0), device_id_type=MESH)
    pl.semaphore_signal(barrier, inc=1, device_id=(gx, gy, other), device_id_type=MESH)

    def tell(at):
        for d in SIDES:
            @pl.when(there(d))
            def _():
                pl.semaphore_signal(
                    near.at[at], inc=1, device_id=(gx + d[0], gy + d[1], 1), device_id_type=MESH)

    def hear(at):
        pl.semaphore_wait(near.at[at], around)

    def spans(d):
        dx, dy = d
        sx = {1: (px, 1), -1: (1, 1), 0: (1, px)}[dx]
        tx = {1: (0, 1), -1: (px + 1, 1), 0: (1, px)}[dx]
        sy = {1: (py, 1), -1: (1, 1), 0: (1, py)}[dy]
        ty = {1: (0, 1), -1: (py + 1, 1), 0: (1, py)}[dy]
        lanes = lambda s: pl.ds(s[0] * nz, s[1] * nz)
        return (pl.ds(*sx), lanes(sy)), (pl.ds(*tx), lanes(ty))

    for d in SIDES:
        tx, tl = spans(d)[1]

        @pl.when(~back(d) & core0)
        def _():
            gate[tx, :, tl] = jnp.zeros((tx.size, cin, tl.size), BF16)

        @pl.when(~back(d) & core1)
        def _():
            acts[tx, :, :, tl] = jnp.zeros((tx.size, 2, ch, tl.size), BF16)

    loads[0].wait()
    for xo in range(px):
        acts[xo + 1, pl.ds(af, 1), :, nz:nz + inner] = (
            act_ref[:, xo].reshape(1, ch, inner))
    pl.semaphore_wait(barrier, around * (1 + af) + 1)

    def act_copy(s, half):
        d = SIDES[s]
        (sx, sl), (tx, tl) = spans(d)
        return pltpu.make_async_remote_copy(
            src_ref=acts.at[sx, half, :, sl], dst_ref=acts.at[tx, half, :, tl],
            send_sem=a_send.at[s], recv_sem=a_recv.at[2 * s + half],
            device_id=(gx + d[0], gy + d[1], 1), device_id_type=MESH)

    def gate_copy(s):
        d = SIDES[s]
        (sx, sl), (tx, tl) = spans(d)
        return pltpu.make_async_remote_copy(
            src_ref=gate.at[sx, :, sl], dst_ref=gate.at[tx, :, tl],
            send_sem=g_send.at[s], recv_sem=g_recv.at[s],
            device_id=(gx + d[0], gy + d[1], 0), device_id_type=MESH)

    def across(at, src, dst):
        return pltpu.make_async_remote_copy(
            src_ref=src, dst_ref=dst, send_sem=c_send.at[at], recv_sem=c_recv.at[at],
            device_id=(gx, gy, other), device_id_type=MESH)

    block = acts.at[pl.ds(1, px), 0, :, pl.ds(nz, inner)]
    act_over = across(0, block, block)
    filt_over = across(1, filt_ref, filt_in)
    bias_over = across(2, bias_ref, bias_in)
    gout_over = across(3, gout_ref, gout_in)
    block = gate.at[pl.ds(1, px), :, pl.ds(nz, inner)]
    gate_over = across(4, block, block)

    def ig_over(xo):
        return pltpu.make_async_remote_copy(
            src_ref=ig_out.at[:, xo], dst_ref=ig_in.at[:, xo],
            send_sem=q_send.at[xo], recv_sem=q_recv.at[xo],
            device_id=(gx, gy, other), device_id_type=MESH)

    order = sorted(range(8), key=lambda s: (SIDES[s][0] == 0) * 2 + (SIDES[s][1] == 0))
    for s in order:
        @pl.when(there(SIDES[s]))
        def _():
            act_copy(s, af).start()

    @pl.when(core0)
    def _():
        act_over.start()

    if rounds > 0:
        @pl.when(core1)
        def _():
            tell(0)

    for load in loads[1:]:
        load.wait()
    filt_over.start()

    lane = lax.broadcasted_iota(jnp.int32, (1, nz), 1)

    def from_below(v):
        return jnp.where(lane == 0, 0.0, pltpu.roll(v, 1, 1))

    def from_above(v):
        return jnp.where(lane == nz - 1, 0.0, pltpu.roll(v, nz - 1, 1))

    step = 2 if py % 2 == 0 else 1
    head = ch
    main, fold = 3 * ch, 3 * ch // 2
    wide = lax.broadcasted_iota(jnp.int32, (1, 2 * cin), 1)

    def two_parts(v):
        high = v.astype(BF16).astype(F32)
        return jnp.where(wide < cin, high, v - high)

    def settle(ref, count, sem):
        block = ref.at[pl.ds(0, count * rows)]
        return pltpu.make_async_copy(block, block, sem)

    low = (n_gx - 1) // 2 * n_gy
    high = low + n_gy if n_gx > 1 else low
    pairs = n_gy // 2
    homes = [(low, high)[b % 2] + b // 2 % pairs * 2 for b in range(n_red)]
    turns = [b // 2 // pairs for b in range(n_red)]
    n_turns = turns[-1] + 1

    def scatter(first, count):
        for b in range(first, first + count):
            for h in range(2):
                chip = homes[b] + h
                block = pack.at[pl.ds((h * n_red + b) * rows, rows)]
                slot = pack_in.at[turns[b], pl.ds(pl.multiple_of(me * rows, 16), rows)]
                came = r_recv.at[turns[b]]

                @pl.when(me == chip)
                def _():
                    pltpu.make_async_copy(block, slot, came).start()

                @pl.when(me != chip)
                def _():
                    pltpu.make_async_remote_copy(
                        src_ref=block, dst_ref=slot, send_sem=r_send, recv_sem=came,
                        device_id=(chip // n_gy, chip % n_gy, 1), device_id_type=MESH).start()

    half = lax.rem(me, 2)
    at_block, has = [], []
    for turn in range(n_turns):
        at, found = jnp.int32(0), jnp.int32(0)
        for b in range(n_red):
            if turns[b] == turn:
                hit = (me - half == homes[b]).astype(jnp.int32)
                at, found = at + b * hit, found + hit
        at_block.append(pl.multiple_of(at * rows, 16))
        has.append(core1 & (found > 0))

    def share(turn, peer):
        own = (half == 1) & (peer == me)
        place = total.at[pl.ds(at_block[turn], rows)]

        @pl.when(own)
        def _():
            pltpu.make_async_copy(mine.at[turn], place, t_recv).start()

        @pl.when(~own)
        def _():
            pltpu.make_async_remote_copy(
                src_ref=mine.at[turn], dst_ref=place, send_sem=t_send.at[turn], recv_sem=t_recv,
                device_id=(peer // n_gy, peer % n_gy, half), device_id_type=MESH).start()

    @pl.when(core1)
    def _():
        for i in range(3):
            for j in range(3):
                w_fwd[j, 3 * ch:6 * ch, i * cin:(i + 1) * cin] = filt_ref[i, j * 3 * ch:(j + 1) * 3 * ch, :]
        for xo in range(px):
            gout[xo, ch:2 * ch] = gout_ref[:, xo].reshape(ch, inner)
        filt_over.wait_recv()
        for i in range(3):
            for j in range(3):
                w_fwd[j, 0:3 * ch, i * cin:(i + 1) * cin] = filt_in[i, j * 3 * ch:(j + 1) * 3 * ch, :]
        bias_over.wait_recv()
        gout_over.wait_recv()
        for xo in range(px):
            gout[xo, 0:ch] = gout_in[:, xo].reshape(ch, inner)
        eye = (lax.broadcasted_iota(jnp.int32, (ch, ch), 0)
               == lax.broadcasted_iota(jnp.int32, (ch, ch), 1))
        bias = [jnp.sum(jnp.where(eye, ref[...], 0.0), axis=1, keepdims=True) for ref in (bias_in, bias_ref)]
        for at in range(1, rounds):
            hear(at - 1)
            tell(at)

        act_over.wait_recv()
        for s in reversed(order):
            @pl.when(back(SIDES[s]))
            def _():
                for h in range(2):
                    act_copy(s, h).wait_recv()

        sums = [jnp.zeros((ch, nz), F32)] * 2
        for xo in range(px):
            for y0 in range(0, py, step):
                acc = None
                for j in range(3):
                    window = acts[xo:xo + 3, :, :, (y0 + j) * nz:(y0 + j + step) * nz]
                    term = jnp.dot(w_fwd[j], window.reshape(3 * cin, step * nz),
                                   preferred_element_type=F32)
                    acc = term if acc is None else acc + term
                for h in range(2):
                    for u in range(step):
                        cut = acc[3 * h * ch:3 * (h + 1) * ch, u * nz:(u + 1) * nz]
                        pre = (cut[ch:2 * ch] + from_below(cut[:ch]) + from_above(cut[2 * ch:])) + bias[h]
                        lanes = slice((y0 + u) * nz, (y0 + u + 1) * nz)
                        squash = 1.0 / (1.0 + jnp.exp(-pre))
                        g = gout[xo, h * ch:(h + 1) * ch, lanes].astype(F32) * squash * (1.0 + pre * (1.0 - squash))
                        rounded = g.astype(BF16)
                        g = rounded.astype(F32)
                        sums[h] = sums[h] + g
                        gate[xo + 1, h * ch:(h + 1) * ch, (y0 + u + 1) * nz:(y0 + u + 2) * nz] = rounded
                        at = 3 * h * ch
                        gate_k[xo, at:at + ch, lanes] = from_above(g).astype(BF16)
                        gate_k[xo, at + ch:at + 2 * ch, lanes] = rounded
                        gate_k[xo, at + 2 * ch:at + 3 * ch, lanes] = from_below(g).astype(BF16)

        used = head + 3 * (main + fold)
        for h in range(2):
            first = h * n_red * rows
            whole = jnp.sum(sums[h], axis=1, keepdims=True) * factor + jnp.zeros((ch, 2 * cin), F32)
            pack[first:first + head, :] = two_parts(whole).astype(BF16)
            if n_red * rows > used:
                pack[first + used:first + n_red * rows, :] = jnp.zeros((n_red * rows - used, 2 * cin), BF16)

        ready = 0
        for j in range(3):
            both = None
            for xo in range(px):
                window = acts[xo:xo + 3, :, :, j * nz:j * nz + inner].reshape(3 * cin, inner)
                term = lax.dot_general(gate_k[xo], window, (((1,), (1,)), ((), ())),
                                       preferred_element_type=F32)
                both = term if both is None else both + term
            both = (both * factor).astype(BF16)
            for h in range(2):
                acc = both[3 * h * ch:3 * (h + 1) * ch]
                base = h * n_red * rows + head + j * (main + fold)
                pack[base:base + main, :] = acc[:, :2 * cin]
                pack[base + main:base + main + fold, 0:cin] = acc[:fold, 2 * cin:]
                pack[base + main:base + main + fold, cin:2 * cin] = acc[fold:, 2 * cin:]
            if j == 0 and rounds > 0:
                hear(rounds - 1)
            done = n_red if j == 2 else (head + (j + 1) * (main + fold)) // rows
            if done > ready:
                scatter(ready, done - ready)
            ready = done

        gate_over.start()
        for s in order:
            @pl.when(there(SIDES[s]))
            def _():
                gate_copy(s).start()

    @pl.when(core0)
    def _():
        bias_over.start()
        gout_over.start()
        filt_over.wait_recv()
        for i in range(3):
            for j in range(3):
                for k in range(3):
                    at = (3 * j + k) * ch
                    to = (2 - i) * cin
                    w_flip[j, to:to + ch, k * cin:(k + 1) * cin] = filt_ref[i, at:at + ch, :]
                    w_flip[j, to + ch:to + cin, k * cin:(k + 1) * cin] = filt_in[i, at:at + ch, :]
        for j in range(3):
            w_bwd[j] = w_flip[j].astype(F32).T.astype(BF16)

        gate_over.wait_recv()
        for s in order:
            @pl.when(back(SIDES[s]))
            def _():
                gate_copy(s).wait_recv()
        for xo in range(px):
            for y0 in range(0, py, step):
                acc = None
                for j in range(3):
                    at = y0 + 2 - j
                    window = gate[xo:xo + 3, :, at * nz:(at + step) * nz].reshape(3 * cin, step * nz)
                    term = jnp.dot(w_bwd[j], window, preferred_element_type=F32)
                    acc = term if acc is None else acc + term
                for u in range(step):
                    cut = acc[:, u * nz:(u + 1) * nz]
                    full = (cut[cin:2 * cin] + from_above(cut[:cin]) + from_below(cut[2 * cin:]))
                    part[xo, :, :, (y0 + u) * nz:(y0 + u + 1) * nz] = full.reshape(2, ch, nz)
            ig_out[:, xo] = part[xo, 1].reshape(ch, py, nz).astype(BF16)
            ig_over(xo).start()
            igrad_ref[:, xo] = part[xo, 0].reshape(ch, py, nz).astype(BF16)

    for turn in range(n_turns):
        @pl.when(has[turn])
        def _():
            settle(pack_in.at[turn], group, r_recv.at[turn]).wait()

            def add(t, v):
                return v + pack_in[turn, pl.ds(pl.multiple_of(t * rows, 16), rows), :].astype(F32)

            summed = pack_in[turn, 0:rows, :].astype(F32)
            if group <= 32:
                for t in range(1, group):
                    summed = add(t, summed)
            else:
                summed = lax.fori_loop(1, group, add, summed)
            both = two_parts(summed + pltpu.roll(summed, cin, 1))
            at = at_block[turn] + lax.broadcasted_iota(jnp.int32, (rows, 1), 0)
            mine[turn] = jnp.where(at < head, both, summed).astype(BF16)
            if group <= 32:
                for peer in range(group):
                    share(turn, peer)
            else:
                lax.fori_loop(0, group, lambda peer, _: share(turn, peer) or 0, 0)

    for s in order:
        @pl.when(there(SIDES[s]))
        def _():
            act_copy(s, af).wait_send()

        @pl.when(there(SIDES[s]) & core1)
        def _():
            gate_copy(s).wait_send()
    filt_over.wait_send()

    @pl.when(core0)
    def _():
        act_over.wait_send()
        bias_over.wait_send()
        gout_over.wait_send()
        for xo in range(px):
            ig_over(xo).wait_send()

    @pl.when(core1)
    def _():
        gate_over.wait_send()
        for xo in range(px):
            ig_over(xo).wait_recv()
        igrad_ref[...] = ig_in[...]

    kept = sum(v.astype(jnp.int32) for v in has)
    for count in range(n_turns + 1):
        @pl.when(core1 & (kept == count))
        def _():
            settle(pack, 2 * n_red - count, r_send).wait()

    for turn in range(n_turns):
        @pl.when(has[turn] & (half == 1))
        def _():
            settle(pack_in.at[turn], group - 1, t_send.at[turn]).wait()

        @pl.when(has[turn] & (half == 0))
        def _():
            settle(pack_in.at[turn], group, t_send.at[turn]).wait()

    settle(total, n_red, t_recv).wait()
    fgrad_ref[...] = total[...]


def unpack(sizes, igrad_ref, packed, igrad_out, fgrad_out, bias_out, taps, bias, sems):
    ch, cin = sizes
    early = pltpu.make_async_copy(igrad_ref, igrad_out, sems.at[0])
    early.start()
    head, main, fold = ch, 3 * ch, 3 * ch // 2
    column = (packed[0:head, :].astype(F32) + pltpu.roll(packed[0:head, :].astype(F32), cin, 1))[:, :1]
    eye = (lax.broadcasted_iota(jnp.int32, (ch, ch), 0)
           == lax.broadcasted_iota(jnp.int32, (ch, ch), 1))
    bias[...] = jnp.sum(jnp.where(eye, column, 0.0), axis=0, keepdims=True)
    small = pltpu.make_async_copy(bias, bias_out, sems.at[1])
    small.start()
    for j in range(3):
        base = head + j * (main + fold)
        block = packed[base:base + main + fold, :].astype(F32)
        at = j * main
        taps[0, at:at + main, :] = block[:main, :cin]
        taps[1, at:at + main, :] = block[:main, cin:]
        taps[2, at:at + fold, :] = block[main:, :cin]
        taps[2, at + fold:at + main, :] = block[main:, cin:]
    large = pltpu.make_async_copy(taps, fgrad_out, sems.at[2])
    large.start()
    early.wait()
    small.wait()
    large.wait()


def per_device(activations, filters, conv_bias, grad_output):
    ch, px, py, nz = activations.shape
    n_gx, n_gy = lax.axis_size("gx"), lax.axis_size("gy")
    group = n_gx * n_gy
    cin = 2 * ch
    inner = py * nz
    factor = 1.0 / math.sqrt(px * n_gx * py * n_gy * nz)
    used = ch + 3 * (3 * ch + 3 * ch // 2)
    rows = 16 * (-(-(used // 16) // 6))
    n_red = -(-used // rows)
    n_turns = (n_red - 1) // 2 // (n_gy // 2) + 1

    vmem = pl.BlockSpec(memory_space=pltpu.VMEM)
    hbm = pl.BlockSpec(memory_space=pltpu.HBM)
    dma = pltpu.SemaphoreType.DMA
    igrad, packed = pl.pallas_call(
        functools.partial(kernel, (n_gx, n_gy, px, py, nz, ch, rows, n_red, factor)),
        out_shape=(jax.ShapeDtypeStruct((ch, px, py, nz), BF16),
                   jax.ShapeDtypeStruct((n_red * rows, 2 * cin), BF16)),
        in_specs=[hbm] * 4,
        out_specs=(vmem, vmem),
        scratch_shapes=[
            pltpu.VMEM((ch, px, py, nz), BF16),
            pltpu.VMEM((3, 9 * ch, cin), BF16),
            pltpu.VMEM((1, ch), F32),
            pltpu.VMEM((ch, px, py, nz), BF16),
            pltpu.VMEM((3, 9 * ch, cin), BF16),
            pltpu.VMEM((1, ch), F32),
            pltpu.VMEM((ch, px, py, nz), BF16),
            dma((4,)),
            pltpu.VMEM((px + 2, 2, ch, (py + 2) * nz), BF16),
            pltpu.VMEM((px + 2, cin, (py + 2) * nz), BF16),
            pltpu.VMEM((px, cin, inner), BF16),
            pltpu.VMEM((px, 3 * cin, inner), BF16),
            pltpu.VMEM((3, 3 * cin, 3 * cin), BF16),
            pltpu.VMEM((3, 3 * cin, 3 * cin), BF16),
            pltpu.VMEM((3, 3 * cin, 3 * cin), BF16),
            pltpu.VMEM((px, 2, ch, inner), F32),
            pltpu.VMEM((ch, px, py, nz), BF16),
            pltpu.VMEM((ch, px, py, nz), BF16),
            pltpu.VMEM((2 * n_red * rows, 2 * cin), BF16),
            pltpu.VMEM((n_turns, group * rows, 2 * cin), BF16),
            pltpu.VMEM((n_turns, rows, 2 * cin), BF16),
            pltpu.VMEM((n_red * rows, 2 * cin), BF16),
            dma((8,)), dma((16,)), dma((5,)), dma((5,)), dma((8,)), dma((8,)),
            dma((px,)), dma((px,)), dma, dma((n_turns,)), dma((n_turns,)), dma,
            pltpu.SemaphoreType.REGULAR((max(1, max(n_gx, n_gy) - 2),)),
        ],
        compiler_params=pltpu.CompilerParams(
            collective_id=0, has_side_effects=True, vmem_limit_bytes=24 * 1024 * 1024),
    )(*[pltpu.with_memory_space_constraint(v, pltpu.HBM) for v in (activations, filters.reshape(3, 9 * ch, cin), conv_bias.reshape(1, ch), grad_output)])
    input_grads, filter_grads, bias_grads = pl.pallas_call(
        functools.partial(unpack, (ch, cin)),
        out_shape=(jax.ShapeDtypeStruct(activations.shape, BF16),
                   jax.ShapeDtypeStruct((3, 9 * ch, cin), F32),
                   jax.ShapeDtypeStruct((1, ch), F32)),
        in_specs=[vmem] * 2,
        out_specs=(hbm,) * 3,
        scratch_shapes=[pltpu.VMEM((3, 9 * ch, cin), F32), pltpu.VMEM((1, ch), F32), dma((3,))],
        compiler_params=pltpu.CompilerParams(vmem_limit_bytes=8 * 1024 * 1024),
    )(igrad, packed)
    return (input_grads, filter_grads.reshape(filters.shape), bias_grads.reshape(ch))


def solution(mesh):
    return jax.shard_map(
        per_device,
        mesh=mesh,
        in_specs=(
            P("af", "gx", "gy", None),
            P(None, None, None, "af", None),
            P("af"),
            P("af", "gx", "gy", None),
        ),
        out_specs=(P("af", "gx", "gy", None), P(None, None, None, "af", None), P("af")),
        check_vma=False,
    )
```

time: 24.8 us -> 21.6 us (0.87)
  the two profiles are of different devices: /device:TPU:0 before, /device:TPU:1 now
where the time goes in v3:
time: 21.6 us; the launch traced here: 21.5 us
  Pallas kernels  20.8 us (96%)
  between operations  0.64 us (3%)
    pallas_call x1, Pallas kernels, per_device(): pl.pallas_call(functools.partial(kernel, (n_gx, n_gy, px, py, nz, ch, row...  19.9 us
    pallas_call x1, Pallas kernels, per_device(): pl.pallas_call(functools.partial(unpack, (ch, cin)), out_shape=(jax.Shape...  0.95 us

profile of v3, /device:TPU:1, one launch (start us, length us, event | category | flops | bytes accessed | tf_op | source)
XLA Modules:
  0.0 21.5 jit_solution(8940369083988465129)
XLA Ops:
  0.6 19.9 %shard_map.67 = (bf16[32,2,8,128]{3,2,1,0:T(8,128)(2,1)S(1)}, bf16[480,128]{1,0:T(8,128)(2,1)S(1)}) custom-call(bf16[32,2,8,128]{3,2,1,0:T(8,128)(2,1)} %act_hbm.1, bf16[3,288,64]{2,1,0:T(8,128)(2,1)} %bitcast.4, f32[1,32]{1,0:T(1,128)} %bitcast.5, bf16[32,2,8,128]{3,2,1,0:T(8,128)(2,1)} %gout_hbm.1), custom_call_target="tpu_custom_call" | custom-call | tf_op jit(solution)/shard_map/pallas_call | solution.py:449
  20.5 0.9 %shard_map.68 = (bf16[32,2,8,128]{3,2,1,0:T(8,128)(2,1)}, f32[3,288,64]{2,1,0:T(8,128)}, f32[1,32]{1,0:T(1,128)}) custom-call(bf16[32,2,8,128]{3,2,1,0:T(8,128)(2,1)S(1)} %get-tuple-element.8.igrad_ref, bf16[480,128]{1,0:T(8,128)(2,1)S(1)} %get-tuple-element.9.packed), custom_call_target="tpu_custom_call" | custom-call | tf_op jit(solution)/shard_map/pallas_call | solution.py:485

commit v4 on v3

--- a/solution.py
+++ b/solution.py
@@ -11,6 +11,7 @@
 MESH = pl.DeviceIdType.MESH
 F32, BF16 = jnp.float32, jnp.bfloat16
 SIDES = [(dx, dy) for dx in (-1, 0, 1) for dy in (-1, 0, 1) if (dx, dy) != (0, 0)]
+EARLY = [s for s, (dx, dy) in enumerate(SIDES) if dx <= 0]
 
 
 def kernel(sizes, act_hbm, filt_hbm, bias_hbm, gout_hbm, igrad_ref, fgrad_ref,
@@ -23,7 +24,7 @@
     other = 1 - af
     group = n_gx * n_gy
     me = gx * n_gy + gy
-    rounds = max(n_gx, n_gy) - 2
+    rounds = max(1, max(n_gx, n_gy) - 2)
     core0, core1 = af == 0, af == 1
 
     loads = [pltpu.make_async_copy(src, dst, load_sem.at[at]) for at, (src, dst) in enumerate((
@@ -39,16 +40,23 @@
 
     barrier = pltpu.get_barrier_semaphore()
     around = sum(there(d).astype(jnp.int32) for d in SIDES)
-    for d in SIDES:
-        @pl.when(there(d))
-        def _():
-            pl.semaphore_signal(
-                barrier, inc=1, device_id=(gx + d[0], gy + d[1], 1), device_id_type=MESH)
-
-        @pl.when(there(d) & core1)
-        def _():
-            pl.semaphore_signal(
-                barrier, inc=1, device_id=(gx + d[0], gy + d[1], 0), device_id_type=MESH)
+    before = sum(there(SIDES[s]).astype(jnp.int32) for s in EARLY)
+
+    def greet(d, core):
+        pl.semaphore_signal(
+            barrier, inc=1, device_id=(gx + d[0], gy + d[1], core), device_id_type=MESH)
+
+    @pl.when(core1)
+    def _():
+        for d in SIDES:
+            @pl.when(there(d))
+            def _():
+                greet(d, 1)
+        for s in EARLY:
+            @pl.when(back(SIDES[s]))
+            def _():
+                greet((-SIDES[s][0], -SIDES[s][1]), 0)
+
     pl.semaphore_signal(barrier, inc=1, device_id=(gx, gy, other), device_id_type=MESH)
 
     def tell(at):
@@ -85,14 +93,14 @@
     for xo in range(px):
         acts[xo + 1, pl.ds(af, 1), :, nz:nz + inner] = (
             act_ref[:, xo].reshape(1, ch, inner))
-    pl.semaphore_wait(barrier, around * (1 + af) + 1)
+    pl.semaphore_wait(barrier, around * af + before * other + 1)
 
     def act_copy(s, half):
         d = SIDES[s]
         (sx, sl), (tx, tl) = spans(d)
         return pltpu.make_async_remote_copy(
             src_ref=acts.at[sx, half, :, sl], dst_ref=acts.at[tx, half, :, tl],
-            send_sem=a_send.at[s], recv_sem=a_recv.at[2 * s + half],
+            send_sem=a_send.at[2 * s + half], recv_sem=a_recv.at[2 * s + half],
             device_id=(gx + d[0], gy + d[1], 1), device_id_type=MESH)
 
     def gate_copy(s):
@@ -123,19 +131,28 @@
             device_id=(gx, gy, other), device_id_type=MESH)
 
     order = sorted(range(8), key=lambda s: (SIDES[s][0] == 0) * 2 + (SIDES[s][1] == 0))
-    for s in order:
-        @pl.when(there(SIDES[s]))
-        def _():
-            act_copy(s, af).start()
-
     @pl.when(core0)
     def _():
+        for s in order:
+            if s in EARLY:
+                @pl.when(there(SIDES[s]))
+                def _():
+                    act_copy(s, 0).start()
         act_over.start()
 
-    if rounds > 0:
-        @pl.when(core1)
-        def _():
-            tell(0)
+    @pl.when(core1)
+    def _():
+        for s in order:
+            @pl.when(there(SIDES[s]))
+            def _():
+                act_copy(s, 1).start()
+        act_over.wait_recv()
+        for s in order:
+            if s not in EARLY:
+                @pl.when(there(SIDES[s]))
+                def _():
+                    act_copy(s, 0).start()
+        tell(0)
 
     for load in loads[1:]:
         load.wait()
@@ -234,7 +251,6 @@
             hear(at - 1)
             tell(at)
 
-        act_over.wait_recv()
         for s in reversed(order):
             @pl.when(back(SIDES[s]))
             def _():
@@ -289,7 +305,7 @@
                 pack[base:base + main, :] = acc[:, :2 * cin]
                 pack[base + main:base + main + fold, 0:cin] = acc[:fold, 2 * cin:]
                 pack[base + main:base + main + fold, cin:2 * cin] = acc[fold:, 2 * cin:]
-            if j == 0 and rounds > 0:
+            if j == 0:
                 hear(rounds - 1)
             done = n_red if j == 2 else (head + (j + 1) * (main + fold)) // rows
             if done > ready:
@@ -362,13 +378,15 @@
                 lax.fori_loop(0, group, lambda peer, _: share(turn, peer) or 0, 0)
 
     for s in order:
-        @pl.when(there(SIDES[s]))
+        @pl.when(there(SIDES[s]) & (core1 | (s in EARLY)))
         def _():
             act_copy(s, af).wait_send()
 
         @pl.when(there(SIDES[s]) & core1)
         def _():
             gate_copy(s).wait_send()
+            if s not in EARLY:
+                act_copy(s, 0).wait_send()
     filt_over.wait_send()
 
     @pl.when(core0)
@@ -475,7 +493,7 @@
             pltpu.VMEM((n_turns, group * rows, 2 * cin), BF16),
             pltpu.VMEM((n_turns, rows, 2 * cin), BF16),
             pltpu.VMEM((n_red * rows, 2 * cin), BF16),
-            dma((8,)), dma((16,)), dma((5,)), dma((5,)), dma((8,)), dma((8,)),
+            dma((16,)), dma((16,)), dma((5,)), dma((5,)), dma((8,)), dma((8,)),
             dma((px,)), dma((px,)), dma, dma((n_turns,)), dma((n_turns,)), dma,
             pltpu.SemaphoreType.REGULAR((max(1, max(n_gx, n_gy) - 2),)),
         ],

time: 21.6 us -> 21.2 us (0.981)
  Pallas kernels: 20.8 us -> 20.4 us
    pallas_call x1, Pallas kernels: 19.9 us -> 19.4 us  [per_device(): pl.pallas_call(functools.partial(kernel, (n_gx, n_gy, px, py, nz, ch, row...]
where the time goes in v4:
time: 21.2 us; the launch traced here: 21 us
  Pallas kernels  20.4 us (96%)
  between operations  0.64 us (3%)
    pallas_call x1, Pallas kernels, per_device(): pl.pallas_call(functools.partial(kernel, (n_gx, n_gy, px, py, nz, ch, row...  19.4 us
    pallas_call x1, Pallas kernels, per_device(): pl.pallas_call(functools.partial(unpack, (ch, cin)), out_shape=(jax.Shape...  0.95 us

profile of v4, /device:TPU:1, one launch (start us, length us, event | category | flops | bytes accessed | tf_op | source)
XLA Modules:
  0.0 21.0 jit_solution(7776211687848597623)
XLA Ops:
  0.6 19.4 %shard_map.67 = (bf16[32,2,8,128]{3,2,1,0:T(8,128)(2,1)S(1)}, bf16[480,128]{1,0:T(8,128)(2,1)S(1)}) custom-call(bf16[32,2,8,128]{3,2,1,0:T(8,128)(2,1)} %act_hbm.1, bf16[3,288,64]{2,1,0:T(8,128)(2,1)} %bitcast.4, f32[1,32]{1,0:T(1,128)} %bitcast.5, bf16[32,2,8,128]{3,2,1,0:T(8,128)(2,1)} %gout_hbm.1), custom_call_target="tpu_custom_call" | custom-call | tf_op jit(solution)/shard_map/pallas_call | solution.py:467
  20.1 0.9 %shard_map.68 = (bf16[32,2,8,128]{3,2,1,0:T(8,128)(2,1)}, f32[3,288,64]{2,1,0:T(8,128)}, f32[1,32]{1,0:T(1,128)}) custom-call(bf16[32,2,8,128]{3,2,1,0:T(8,128)(2,1)S(1)} %get-tuple-element.8.igrad_ref, bf16[480,128]{1,0:T(8,128)(2,1)S(1)} %get-tuple-element.9.packed), custom_call_target="tpu_custom_call" | custom-call | tf_op jit(solution)/shard_map/pallas_call | solution.py:503

commit v5 on v4

--- a/solution.py
+++ b/solution.py
@@ -14,7 +14,7 @@
 EARLY = [s for s, (dx, dy) in enumerate(SIDES) if dx <= 0]
 
 
-def kernel(sizes, act_hbm, filt_hbm, bias_hbm, gout_hbm, igrad_ref, fgrad_ref,
+def kernel(sizes, act_hbm, filt_hbm, bias_hbm, gout_hbm, igrad_ref, taps_ref, bias_out,
            act_ref, filt_ref, bias_ref, gout_ref, filt_in, bias_in, gout_in, load_sem, acts, gate, gout, gate_k, w_fwd, w_flip, w_bwd, part, ig_out, ig_in, pack, pack_in, mine, total,
            a_send, a_recv, c_send, c_recv, g_send, g_recv, q_send, q_recv, r_send, r_recv, t_send, t_recv, near):
     n_gx, n_gy, px, py, nz, ch, rows, n_red, factor = sizes
@@ -27,37 +27,37 @@
     rounds = max(1, max(n_gx, n_gy) - 2)
     core0, core1 = af == 0, af == 1
 
+    def there(d):
+        return (gx + d[0] >= 0) & (gx + d[0] < n_gx) & (gy + d[1] >= 0) & (gy + d[1] < n_gy)
+
+    def back(d):
+        return there((-d[0], -d[1]))
+
+    barrier = pltpu.get_barrier_semaphore()
+    around = sum(there(d).astype(jnp.int32) for d in SIDES)
+    before = sum(there(SIDES[s]).astype(jnp.int32) for s in EARLY)
+
+    def greet(d, core):
+        pl.semaphore_signal(
+            barrier, inc=1, device_id=(gx + d[0], gy + d[1], core), device_id_type=MESH)
+
+    @pl.when(core1)
+    def _():
+        for d in SIDES:
+            @pl.when(there(d))
+            def _():
+                greet(d, 1)
+        for s in EARLY:
+            @pl.when(back(SIDES[s]))
+            def _():
+                greet((-SIDES[s][0], -SIDES[s][1]), 0)
+
+    pl.semaphore_signal(barrier, inc=1, device_id=(gx, gy, other), device_id_type=MESH)
+
     loads = [pltpu.make_async_copy(src, dst, load_sem.at[at]) for at, (src, dst) in enumerate((
         (act_hbm, act_ref), (filt_hbm, filt_ref), (bias_hbm, bias_ref), (gout_hbm, gout_ref)))]
     for load in loads:
         load.start()
-
-    def there(d):
-        return (gx + d[0] >= 0) & (gx + d[0] < n_gx) & (gy + d[1] >= 0) & (gy + d[1] < n_gy)
-
-    def back(d):
-        return there((-d[0], -d[1]))
-
-    barrier = pltpu.get_barrier_semaphore()
-    around = sum(there(d).astype(jnp.int32) for d in SIDES)
-    before = sum(there(SIDES[s]).astype(jnp.int32) for s in EARLY)
-
-    def greet(d, core):
-        pl.semaphore_signal(
-            barrier, inc=1, device_id=(gx + d[0], gy + d[1], core), device_id_type=MESH)
-
-    @pl.when(core1)
-    def _():
-        for d in SIDES:
-            @pl.when(there(d))
-            def _():
-                greet(d, 1)
-        for s in EARLY:
-            @pl.when(back(SIDES[s]))
-            def _():
-                greet((-SIDES[s][0], -SIDES[s][1]), 0)
-
-    pl.semaphore_signal(barrier, inc=1, device_id=(gx, gy, other), device_id_type=MESH)
 
     def tell(at):
         for d in SIDES:
@@ -188,7 +188,7 @@
 
     def scatter(first, count):
         for b in range(first, first + count):
-            for h in range(2):
+            for h in (1, 0):
                 chip = homes[b] + h
                 block = pack.at[pl.ds((h * n_red + b) * rows, rows)]
                 slot = pack_in.at[turns[b], pl.ds(pl.multiple_of(me * rows, 16), rows)]
@@ -215,19 +215,25 @@
         at_block.append(pl.multiple_of(at * rows, 16))
         has.append(core1 & (found > 0))
 
+    def give(turn, peer):
+        pltpu.make_async_remote_copy(
+            src_ref=mine.at[turn], dst_ref=total.at[pl.ds(at_block[turn], rows)],
+            send_sem=t_send.at[turn], recv_sem=t_recv.at[turn],
+            device_id=(peer // n_gy, peer % n_gy, half), device_id_type=MESH).start()
+
     def share(turn, peer):
-        own = (half == 1) & (peer == me)
-        place = total.at[pl.ds(at_block[turn], rows)]
-
-        @pl.when(own)
-        def _():
-            pltpu.make_async_copy(mine.at[turn], place, t_recv).start()
-
-        @pl.when(~own)
-        def _():
-            pltpu.make_async_remote_copy(
-                src_ref=mine.at[turn], dst_ref=place, send_sem=t_send.at[turn], recv_sem=t_recv,
-                device_id=(peer // n_gy, peer % n_gy, half), device_id_type=MESH).start()
+        @pl.when(peer != me)
+        def _():
+            give(turn, peer)
+
+    def keep(turn):
+        @pl.when(half == 1)
+        def _():
+            pltpu.make_async_copy(mine.at[turn], total.at[pl.ds(at_block[turn], rows)], t_recv.at[turn]).start()
+
+        @pl.when(half == 0)
+        def _():
+            give(turn, me)
 
     @pl.when(core1)
     def _():
@@ -372,10 +378,11 @@
             at = at_block[turn] + lax.broadcasted_iota(jnp.int32, (rows, 1), 0)
             mine[turn] = jnp.where(at < head, both, summed).astype(BF16)
             if group <= 32:
-                for peer in range(group):
+                for peer in sorted(range(group), key=lambda v: (v // n_gy, (0, 2, 1, 3)[v % n_gy] if n_gy == 4 else v)):
                     share(turn, peer)
             else:
                 lax.fori_loop(0, group, lambda peer, _: share(turn, peer) or 0, 0)
+            keep(turn)
 
     for s in order:
         @pl.when(there(SIDES[s]) & (core1 | (s in EARLY)))
@@ -419,34 +426,32 @@
         def _():
             settle(pack_in.at[turn], group, t_send.at[turn]).wait()
 
-    settle(total, n_red, t_recv).wait()
-    fgrad_ref[...] = total[...]
-
-
-def unpack(sizes, igrad_ref, packed, igrad_out, fgrad_out, bias_out, taps, bias, sems):
-    ch, cin = sizes
-    early = pltpu.make_async_copy(igrad_ref, igrad_out, sems.at[0])
-    early.start()
-    head, main, fold = ch, 3 * ch, 3 * ch // 2
-    column = (packed[0:head, :].astype(F32) + pltpu.roll(packed[0:head, :].astype(F32), cin, 1))[:, :1]
-    eye = (lax.broadcasted_iota(jnp.int32, (ch, ch), 0)
-           == lax.broadcasted_iota(jnp.int32, (ch, ch), 1))
-    bias[...] = jnp.sum(jnp.where(eye, column, 0.0), axis=0, keepdims=True)
-    small = pltpu.make_async_copy(bias, bias_out, sems.at[1])
-    small.start()
-    for j in range(3):
-        base = head + j * (main + fold)
-        block = packed[base:base + main + fold, :].astype(F32)
-        at = j * main
-        taps[0, at:at + main, :] = block[:main, :cin]
-        taps[1, at:at + main, :] = block[:main, cin:]
-        taps[2, at:at + fold, :] = block[main:, :cin]
-        taps[2, at + fold:at + main, :] = block[main:, cin:]
-    large = pltpu.make_async_copy(taps, fgrad_out, sems.at[2])
-    large.start()
-    early.wait()
-    small.wait()
-    large.wait()
+    done = 0
+    for turn in range(n_turns):
+        settle(total, turns.count(turn), t_recv.at[turn]).wait()
+        if turn == 0:
+            lead = total[0:head, :].astype(F32)
+            column = (lead + pltpu.roll(lead, cin, 1))[:, :1]
+            eye = (lax.broadcasted_iota(jnp.int32, (ch, ch), 0)
+                   == lax.broadcasted_iota(jnp.int32, (ch, ch), 1))
+            bias_out[...] = jnp.sum(jnp.where(eye, column, 0.0), axis=0, keepdims=True)
+        known = rows * sum(v <= turn for v in turns)
+        while done < 3 and head + (done + 1) * (main + fold) <= known:
+            base, at = head + done * (main + fold), done * main
+            block = total[base:base + main + fold, :].astype(F32)
+            taps_ref[0, at:at + main, :] = block[:main, :cin]
+            taps_ref[1, at:at + main, :] = block[:main, cin:]
+            taps_ref[2, at:at + fold, :] = block[main:, :cin]
+            taps_ref[2, at + fold:at + main, :] = block[main:, cin:]
+            done += 1
+
+
+def write(*refs):
+    copies = [pltpu.make_async_copy(refs[at], refs[3 + at], refs[6].at[at]) for at in range(3)]
+    for copy in copies:
+        copy.start()
+    for copy in copies:
+        copy.wait()
 
 
 def per_device(activations, filters, conv_bias, grad_output):
@@ -464,12 +469,13 @@
     vmem = pl.BlockSpec(memory_space=pltpu.VMEM)
     hbm = pl.BlockSpec(memory_space=pltpu.HBM)
     dma = pltpu.SemaphoreType.DMA
-    igrad, packed = pl.pallas_call(
+    parts = pl.pallas_call(
         functools.partial(kernel, (n_gx, n_gy, px, py, nz, ch, rows, n_red, factor)),
         out_shape=(jax.ShapeDtypeStruct((ch, px, py, nz), BF16),
-                   jax.ShapeDtypeStruct((n_red * rows, 2 * cin), BF16)),
+                   jax.ShapeDtypeStruct((3, 9 * ch, cin), F32),
+                   jax.ShapeDtypeStruct((1, ch), F32)),
         in_specs=[hbm] * 4,
-        out_specs=(vmem, vmem),
+        out_specs=(vmem,) * 3,
         scratch_shapes=[
             pltpu.VMEM((ch, px, py, nz), BF16),
             pltpu.VMEM((3, 9 * ch, cin), BF16),
@@ -494,22 +500,22 @@
             pltpu.VMEM((n_turns, rows, 2 * cin), BF16),
             pltpu.VMEM((n_red * rows, 2 * cin), BF16),
             dma((16,)), dma((16,)), dma((5,)), dma((5,)), dma((8,)), dma((8,)),
-            dma((px,)), dma((px,)), dma, dma((n_turns,)), dma((n_turns,)), dma,
+            dma((px,)), dma((px,)), dma, dma((n_turns,)), dma((n_turns,)), dma((n_turns,)),
             pltpu.SemaphoreType.REGULAR((max(1, max(n_gx, n_gy) - 2),)),
         ],
         compiler_params=pltpu.CompilerParams(
             collective_id=0, has_side_effects=True, vmem_limit_bytes=24 * 1024 * 1024),
     )(*[pltpu.with_memory_space_constraint(v, pltpu.HBM) for v in (activations, filters.reshape(3, 9 * ch, cin), conv_bias.reshape(1, ch), grad_output)])
     input_grads, filter_grads, bias_grads = pl.pallas_call(
-        functools.partial(unpack, (ch, cin)),
+        write,
         out_shape=(jax.ShapeDtypeStruct(activations.shape, BF16),
                    jax.ShapeDtypeStruct((3, 9 * ch, cin), F32),
                    jax.ShapeDtypeStruct((1, ch), F32)),
-        in_specs=[vmem] * 2,
+        in_specs=[vmem] * 3,
         out_specs=(hbm,) * 3,
-        scratch_shapes=[pltpu.VMEM((3, 9 * ch, cin), F32), pltpu.VMEM((1, ch), F32), dma((3,))],
+        scratch_shapes=[dma((3,))],
         compiler_params=pltpu.CompilerParams(vmem_limit_bytes=8 * 1024 * 1024),
-    )(igrad, packed)
+    )(*parts)
     return (input_grads, filter_grads.reshape(filters.shape), bias_grads.reshape(ch))
 
 

time: 21.2 us -> 21 us (level)
  no operation moved by 1% of the time
where the time goes in v5:
time: 21 us; the launch traced here: 20.9 us
  Pallas kernels  20.2 us (96%)
  between operations  0.64 us (3%)
    pallas_call x1, Pallas kernels, per_device(): pl.pallas_call(functools.partial(kernel, (n_gx, n_gy, px, py, nz, ch, row...  19.4 us
    pallas_call x1, Pallas kernels, per_device(): pl.pallas_call(write, out_shape=(jax.ShapeDtypeStruct(activations.shape,...  0.84 us

profile of v5, /device:TPU:1, one launch (start us, length us, event | category | flops | bytes accessed | tf_op | source)
XLA Modules:
  0.0 20.9 jit_solution(7483724391852320934)
XLA Ops:
  0.6 19.4 %shard_map.67 = (bf16[32,2,8,128]{3,2,1,0:T(8,128)(2,1)S(1)}, f32[3,288,64]{2,1,0:T(8,128)S(1)}, f32[1,32]{1,0:T(1,128)S(1)}) custom-call(bf16[32,2,8,128]{3,2,1,0:T(8,128)(2,1)} %act_hbm.1, bf16[3,288,64]{2,1,0:T(8,128)(2,1)} %bitcast.4, f32[1,32]{1,0:T(1,128)} %bitcast.5, bf16[32,2,8,128]{3,2,1,0:T(8,128)(2,1)} %gout_hbm.1), custom_call_target="tpu_custom_call" | custom-call | tf_op jit(solution)/shard_map/pallas_call | solution.py:472
  20.0 0.8 %shard_map.68 = (bf16[32,2,8,128]{3,2,1,0:T(8,128)(2,1)}, f32[3,288,64]{2,1,0:T(8,128)}, f32[1,32]{1,0:T(1,128)}) custom-call(bf16[32,2,8,128]{3,2,1,0:T(8,128)(2,1)S(1)} %get-tuple-element.9.refs_0_, f32[3,288,64]{2,1,0:T(8,128)S(1)} %get-tuple-element.10.refs_1_, f32[1,32]{1,0:T(1,128)S(1)} %get-tuple-element.11.refs_2_), custom_call_target="tpu_custom_call" | custom-call | tf_op jit(solution)/shard_map/pallas_call | solution.py:509

commit v6 on v5

--- a/solution.py
+++ b/solution.py
@@ -130,7 +130,7 @@
             send_sem=q_send.at[xo], recv_sem=q_recv.at[xo],
             device_id=(gx, gy, other), device_id_type=MESH)
 
-    order = sorted(range(8), key=lambda s: (SIDES[s][0] == 0) * 2 + (SIDES[s][1] == 0))
+    order = sorted(range(8), key=lambda s: (SIDES[s][0] != 0 and SIDES[s][1] == 0, SIDES[s][0] == 0))
     @pl.when(core0)
     def _():
         for s in order:

time: 21 us -> 21 us (level)
  no operation moved by 1% of the time
where the time goes in v6:
time: 21 us; the launch traced here: 20.9 us
  Pallas kernels  20.2 us (96%)
  between operations  0.64 us (3%)
    pallas_call x1, Pallas kernels, per_device(): pl.pallas_call(functools.partial(kernel, (n_gx, n_gy, px, py, nz, ch, row...  19.4 us
    pallas_call x1, Pallas kernels, per_device(): pl.pallas_call(write, out_shape=(jax.ShapeDtypeStruct(activations.shape,...  0.84 us

profile of v6, /device:TPU:1, one launch (start us, length us, event | category | flops | bytes accessed | tf_op | source)
XLA Modules:
  0.0 20.9 jit_solution(16762432078672934993)
XLA Ops:
  0.6 19.4 %shard_map.67 = (bf16[32,2,8,128]{3,2,1,0:T(8,128)(2,1)S(1)}, f32[3,288,64]{2,1,0:T(8,128)S(1)}, f32[1,32]{1,0:T(1,128)S(1)}) custom-call(bf16[32,2,8,128]{3,2,1,0:T(8,128)(2,1)} %act_hbm.1, bf16[3,288,64]{2,1,0:T(8,128)(2,1)} %bitcast.4, f32[1,32]{1,0:T(1,128)} %bitcast.5, bf16[32,2,8,128]{3,2,1,0:T(8,128)(2,1)} %gout_hbm.1), custom_call_target="tpu_custom_call" | custom-call | tf_op jit(solution)/shard_map/pallas_call | solution.py:472
  20.0 0.8 %shard_map.68 = (bf16[32,2,8,128]{3,2,1,0:T(8,128)(2,1)}, f32[3,288,64]{2,1,0:T(8,128)}, f32[1,32]{1,0:T(1,128)}) custom-call(bf16[32,2,8,128]{3,2,1,0:T(8,128)(2,1)S(1)} %get-tuple-element.9.refs_0_, f32[3,288,64]{2,1,0:T(8,128)S(1)} %get-tuple-element.10.refs_1_, f32[1,32]{1,0:T(1,128)S(1)} %get-tuple-element.11.refs_2_), custom_call_target="tpu_custom_call" | custom-call | tf_op jit(solution)/shard_map/pallas_call | solution.py:509
